TPU v7x, 1024 devices: a whole 4x8x16 slice. The times are simulated.
1024 devices in a mesh: blk: 16 (over x, y_lo, core), dp: 64 (over z, y_hi).
Axes of the slice: x: 4, y: 8 (y_hi: 4, y_lo: 2; y = y_hi * 2 + y_lo), z: 16, core: 2. Of those that a mesh axis runs over, the one named last changes fastest.
Arguments:
- patches: bfloat16 [16, 64, 64, 12, 1152], P('blk', 'dp'), may hold values from -8 to 8
- counts: int32 [16, 64, 64], P('blk'), may hold values from 0 to 12, as said below
- w_qkv: bfloat16 [1152, 1728], replicated, may hold values from -0.1875 to 0.1875
- w_out: bfloat16 [576, 1152], replicated, may hold values from -0.25 to 0.25
- text_rows: bfloat16 [64, 768, 1152], P('dp', 'blk'), may hold values from -160 to 160
- labels: int32 [64, 768], P('dp', 'blk'), may hold values from 0 to 767, each once within a row
Outputs:
- losses: float32 [64, 768], P('dp', 'blk')
- d_pooled: float32 [64, 768, 1152], P('dp', 'blk')
- d_texts: float32 [64, 768, 1152], P('dp', 'blk')
Inputs may be any that keep to these rules, and one draw needn't show every extreme that they name: `counts`: A device sends at most one image to each device of its dp group; every device receives exactly 48 images with exactly 384 patches in all, and one of them has exactly 12 patches; a sent image has at least 4 patches. `labels`: each row is a permutation of the group's text indices.
All inputs are finite; a program needn't handle non-finite values.
Results may differ from a plain program's by a relative error of at most 0.0046.
Values may be sent and summed in bfloat16 or wider, within the bound.
A program may use at most 64 MiB of HBM per device.

v0:
```python
import functools

import jax
import jax.numpy as jnp
from jax import lax
from jax.experimental import pallas as pl
from jax.experimental.pallas import tpu as pltpu
from jax.sharding import PartitionSpec as P

HEADS = 8
HEAD_DIM = 72
SUBGROUP = 16

logit_scale = 16.0
logit_bias = -4.0
epsilon = 1e-06

NT = (((1,), (1,)), ((), ()))
MESH = pl.DeviceIdType.MESH
PIECE = 16


def column_of(row):
    n = row.shape[1]
    eye = lax.broadcasted_iota(jnp.int32, (n, n), 0) == lax.broadcasted_iota(jnp.int32, (n, n), 1)
    return jnp.sum(jnp.where(eye, row, jnp.zeros_like(row)), axis=1, keepdims=True)


def row_of(column):
    n = column.shape[0]
    eye = lax.broadcasted_iota(jnp.int32, (n, n), 0) == lax.broadcasted_iota(jnp.int32, (n, n), 1)
    return jnp.sum(jnp.where(eye, column, jnp.zeros_like(column)), axis=0, keepdims=True)


def halves(values):
    high = values.astype(jnp.bfloat16)
    low = (values - high.astype(jnp.float32)).astype(jnp.bfloat16)
    return jnp.concatenate([high, low], axis=0)


def split_dot(values, other):
    rows = values.shape[0]
    both = jnp.dot(halves(values), other, preferred_element_type=jnp.float32)
    return both[:rows] + both[rows:]


def inverse_norms(values):
    return lax.rsqrt(jnp.sum(values * values, axis=-1, keepdims=True) + epsilon)


def pair_terms(own, own_scale, others, matching):
    others_scale = row_of(inverse_norms(others.astype(jnp.float32)))
    products = lax.dot_general(own, others, NT, preferred_element_type=jnp.float32)
    logits = logit_scale * (products * own_scale * others_scale) + logit_bias
    sign = jnp.where(matching, 1.0, -1.0)
    margins = -sign * logits
    slopes = -sign / (1.0 + jnp.exp(-margins))
    return margins, slopes * others_scale


def tangent(own, own_scale, gradient):
    unit = own.astype(jnp.float32) * own_scale
    return (gradient - unit * jnp.sum(unit * gradient, axis=-1, keepdims=True)) * own_scale


def main_kernel(
    patch_hbm, counts_ref, wt_hbm, wo_hbm, text_ref, label_ref, img_ref, loss_ref, img_grad_ref, text_grad_ref,
    patch_ref, wt_ref, wo_ref, normed_ref, packed_ref, mean_ref, pool_ref, wide_ref, sent_ref, arrived_ref,
    texts_ref, labels_ref, gathered_ref,
    load_sems, send_sem, recv_sem, text_send_sems, text_recv_sems, send_sems, recv_sems,
):
    blocks = texts_ref.shape[0]
    place = lax.axis_index("blk")
    sibling = place + 1 - 2 * lax.rem(place, 2)

    def across(block):
        return block + 2 - 4 * lax.rem(lax.div(block, 2), 2)

    beside = across(place)
    right, left, opposite = (lax.rem(place + 4 * step, blocks) for step in (1, 3, 2))
    peers = (opposite, across(opposite), across(right), across(left), right, left, beside)
    mirror = (0, 1, 3, 2, 5, 4, 6)
    cap, dests, width = patch_ref.shape
    inner = HEADS * HEAD_DIM
    rows = cap * SUBGROUP
    groups = dests // SUBGROUP
    images = img_ref.shape[0]
    half = sent_ref.shape[2]
    me = lax.axis_index("dp")

    loads = [pltpu.make_async_copy(patch_hbm, patch_ref, load_sems.at[0])]
    for p in range(3):
        span = pl.ds(p * inner, inner)
        loads.append(pltpu.make_async_copy(wt_hbm.at[span], wt_ref.at[span], load_sems.at[1 + p]))
    loads.append(pltpu.make_async_copy(wo_hbm, wo_ref, load_sems.at[4]))
    for load in loads:
        load.start()

    barrier = pltpu.get_barrier_semaphore()

    def greet(step, carry):
        pl.semaphore_signal(barrier, inc=1, device_id={"dp": lax.rem(me + step, dests)}, device_id_type=MESH)
        return carry

    lax.fori_loop(1, dests, greet, 0)
    for neighbour in (sibling,) + peers:
        pl.semaphore_signal(barrier, inc=1, device_id={"blk": neighbour}, device_id_type=MESH)

    texts_ref[place] = text_ref[...]
    label_row = jnp.concatenate([label_ref[...], jnp.zeros((1, 128 - images), jnp.int32)], axis=1)
    labels_ref[place] = jnp.broadcast_to(label_row, labels_ref.shape[1:])

    lengths_row = counts_ref[pl.ds(me, 1), :]
    id_row = lax.broadcasted_iota(jnp.int32, (SUBGROUP, dests), 1)
    id_column = lax.broadcasted_iota(jnp.int32, (SUBGROUP, dests), 0)
    order = [lax.rem(lax.div(me, SUBGROUP) + step, groups) for step in (2, 1, 3, 0)[4 - groups :]]
    lengths = [
        jnp.sum(jnp.where(id_row == id_column + g * SUBGROUP, lengths_row, 0), axis=1, keepdims=True) for g in order
    ]
    inverse_lengths = [1.0 / jnp.maximum(length, 1).astype(jnp.float32) for length in lengths]

    loads[0].wait()
    for k, g in enumerate(order):
        total = jnp.zeros((SUBGROUP, width), jnp.float32)
        for r in range(cap):
            block = patch_ref[r, pl.ds(pl.multiple_of(g * SUBGROUP, SUBGROUP), SUBGROUP), :].astype(jnp.float32)
            centred = block - jnp.mean(block, axis=-1, keepdims=True)
            spread = jnp.mean(centred * centred, axis=-1, keepdims=True)
            start = k * rows + r * SUBGROUP
            normed_ref[start : start + SUBGROUP, :] = (centred * lax.rsqrt(spread + epsilon)).astype(jnp.bfloat16)
            total = total + jnp.where(lengths[k] > r, block, 0.0)
        mean_ref[k * SUBGROUP : (k + 1) * SUBGROUP, :] = total * inverse_lengths[k]

    for p in range(3):
        loads[1 + p].wait()
        packed_ref[p] = lax.dot_general(
            normed_ref[...], wt_ref[p * inner : (p + 1) * inner, :], NT, preferred_element_type=jnp.float32
        ).astype(jnp.bfloat16)
    loads[4].wait()

    query_id = lax.broadcasted_iota(jnp.int32, (rows, rows), 0)
    key_id = lax.broadcasted_iota(jnp.int32, (rows, rows), 1)
    same_image = query_id % SUBGROUP == key_id % SUBGROUP
    lane_image = lax.broadcasted_iota(jnp.int32, (SUBGROUP, rows), 1) % SUBGROUP
    pick = lax.broadcasted_iota(jnp.int32, (SUBGROUP, rows), 0) == lane_image
    head_of = lax.broadcasted_iota(jnp.int32, (HEADS, 1, inner), 2)
    head_start = lax.broadcasted_iota(jnp.int32, (HEADS, 1, inner), 0) * HEAD_DIM
    head_mask = ((head_of >= head_start) & (head_of < head_start + HEAD_DIM)).astype(jnp.float32)
    column_id = lax.broadcasted_iota(jnp.int32, (1, inner), 1)
    ones = jnp.ones((rows, 128), jnp.bfloat16)
    largest = float(jnp.finfo(jnp.bfloat16).max)

    def pool_group(k):
        key_lengths = jnp.sum(jnp.where(pick, lengths[k], 0), axis=0, keepdims=True)
        query_lengths = jnp.concatenate([lengths[k]] * cap, axis=0)
        query_live = query_id[:, :1] // SUBGROUP < query_lengths
        usable = same_image & (key_id // SUBGROUP < key_lengths) & query_live
        query_share = jnp.concatenate([inverse_lengths[k]] * cap, axis=0)
        group_rows = slice(k * rows, (k + 1) * rows)
        picked = []
        for h in range(HEADS):
            low = h * HEAD_DIM // 128 * 128
            high = min(-(-(h + 1) * HEAD_DIM // 128) * 128, inner)
            window = (column_id[:, low:high] >= h * HEAD_DIM) & (column_id[:, low:high] < (h + 1) * HEAD_DIM)
            queries = packed_ref[0, group_rows, low:high] * window.astype(jnp.bfloat16)
            keys = packed_ref[1, group_rows, low:high]
            scores = lax.dot_general(queries, keys, NT, preferred_element_type=jnp.float32) * HEAD_DIM ** (-0.5)
            raised = jnp.where(usable, jnp.minimum(jnp.exp(scores), largest), 0.0).astype(jnp.bfloat16)
            denominators = jnp.dot(raised, ones, preferred_element_type=jnp.float32)
            share = jnp.where(query_live, query_share / denominators, 0.0)
            share = jnp.concatenate([share, share[:, : rows - 128]], axis=1)
            weights = raised.astype(jnp.float32) * share
            picked.append(jnp.sum(weights.reshape(cap, SUBGROUP, rows), axis=0))
        stacked = jnp.concatenate(picked, axis=0).astype(jnp.bfloat16)
        mixed = jnp.dot(stacked, packed_ref[2, group_rows, :], preferred_element_type=jnp.float32)
        return jnp.sum(mixed.reshape(HEADS, SUBGROUP, inner) * head_mask, axis=0)

    text_copies, label_copies = [], []

    def pass_text(k, block, to):
        for ref, sems, copies in ((texts_ref, 0, text_copies), (labels_ref, 15, label_copies)):
            spot = ref.at[block]
            copy = pltpu.make_async_remote_copy(
                spot, spot, text_send_sems.at[sems + k], text_recv_sems.at[sems + k],
                device_id={"blk": to}, device_id_type=MESH,
            )
            copy.start()
            copies.append(copy)

    for members in (range(groups - 1), range(groups - 1, groups)):
        for k in members:
            pool_ref[k * SUBGROUP : (k + 1) * SUBGROUP, :] = pool_group(k)
        span = slice(members[0] * SUBGROUP, (members[-1] + 1) * SUBGROUP)
        result = mean_ref[span, :] + split_dot(pool_ref[span, :], wo_ref[...])
        wide_ref[span, 0, :] = result[:, :half]
        filler = jnp.zeros((result.shape[0], 2 * half - width), jnp.float32)
        wide_ref[span, 1, :] = jnp.concatenate([result[:, half:], filler], axis=1)
        if members[0] == 0:
            pl.semaphore_wait(barrier, dests - 1 + 1 + len(peers))
        for k in members:
            base = order[k] * SUBGROUP
            sent_ref[pl.ds(base, SUBGROUP)] = wide_ref[k * SUBGROUP : (k + 1) * SUBGROUP].astype(jnp.bfloat16)

            def send(step, carry, base=base):
                to = base + lax.rem(me + step, SUBGROUP)
                pltpu.make_async_remote_copy(
                    sent_ref.at[to], arrived_ref.at[me], send_sem, recv_sem, device_id={"dp": to}, device_id_type=MESH
                ).start()
                return carry

            lax.fori_loop(1 if k == groups - 1 else 0, SUBGROUP, send, 0)
        if members[0] == 0:
            for k, to in enumerate(peers + (sibling,)):
                pass_text(k, place, to)
    arrived_ref[me] = sent_ref[me]

    lane = lax.broadcasted_iota(jnp.int32, (dests, dests), 1)
    sublane = lax.broadcasted_iota(jnp.int32, (dests, dests), 0)
    intake = jnp.sum(jnp.where(lane == me, counts_ref[...], 0), axis=1, keepdims=True)
    living = (intake > 0).astype(jnp.int32)
    living_row = row_of(living)
    ranking_row = jnp.sum(jnp.where(sublane < lane, living, 0), axis=0, keepdims=True)
    image_id = lax.broadcasted_iota(jnp.int32, (images, dests), 0)
    chooser = ((ranking_row == image_id) & (living_row > 0)).astype(jnp.bfloat16)

    batch = 4
    wide = batch * images

    pltpu.make_async_remote_copy(
        sent_ref.at[pl.ds(0, dests - 1)], arrived_ref.at[pl.ds(0, dests - 1)], send_sem, recv_sem,
        device_id={"dp": lax.rem(me + 1, dests)}, device_id_type=MESH,
    ).wait()
    wide_ref[...] = arrived_ref[...].astype(jnp.float32)
    for low, high, lane_half in ((0, half, 0), (half, width, 1)):
        values = wide_ref[:, lane_half, : high - low].astype(jnp.bfloat16)
        chosen = jnp.dot(chooser, values, preferred_element_type=jnp.float32)
        img_ref[:, low:high] = chosen.astype(img_ref.dtype)

    gathered_ref[place] = img_ref[...]

    pieces = images // PIECE
    started = []

    def put(stage, c, block, to):
        span = pl.ds(c * PIECE, PIECE)
        spot = gathered_ref.at[block, span]
        k = stage * pieces + c
        copy = pltpu.make_async_remote_copy(
            img_ref.at[span] if block is place else spot, spot, send_sems.at[k], recv_sems.at[k],
            device_id={"blk": to}, device_id_type=MESH,
        )
        copy.start()
        started.append(copy)
        return copy

    own = img_ref[...]
    own_scale = inverse_norms(own.astype(jnp.float32))
    text = text_ref[...]
    text_scale = inverse_norms(text.astype(jnp.float32))
    label_column = column_of(label_ref[...])
    lane_id = lax.broadcasted_iota(jnp.int32, (images, wide), 1)
    text_id = place * images + lax.broadcasted_iota(jnp.int32, (images, wide), 0)

    def image_batch(q):
        others = texts_ref[batch * q : batch * (q + 1)].reshape(wide, width)
        matching = label_column == lane_id + q * wide
        margins, weights = pair_terms(own, own_scale, others, matching)
        losses = jnp.maximum(margins, 0.0) + jnp.log1p(jnp.exp(-jnp.abs(margins)))
        gradient = split_dot(weights, others)
        if q == 0:
            img_grad_ref[...] = gradient
            return losses
        img_grad_ref[...] += gradient
        return losses

    def text_batch(head, is_first):
        first = lax.div(head, batch) * batch
        others = gathered_ref[pl.ds(first, batch)].reshape(wide, width)
        labels = [labels_ref[first + i, 0:1, :images] for i in range(batch)]
        matching = jnp.concatenate(labels, axis=1) == text_id
        _, weights = pair_terms(text, text_scale, others, matching)
        gradient = split_dot(weights, others)
        if is_first:
            text_grad_ref[...] = gradient
        else:
            text_grad_ref[...] += gradient

    each = range(pieces)
    to_right = [put(0, c, place, right) for c in each]
    to_left = [put(1, c, place, left) for c in each]
    to_beside = [put(2, c, place, beside) for c in each]
    to_sibling = [put(3, c, place, sibling) for c in each]
    for k in (6, 4, 5, 2, 3, 0, 1):
        text_copies[k].wait_recv()
        label_copies[k].wait_recv()
        pass_text(8 + k, peers[mirror[k]], sibling)

    sibling_waits = []
    beside_right, beside_left, opposite_own = [], [], []
    for c in each:
        to_beside[c].wait_recv()
        beside_right.append(put(4, c, beside, right))
        beside_left.append(put(5, c, beside, left))
        to_right[c].wait_recv()
        to_left[c].wait_recv()
        opposite_own.append(put(6, c, right, left) if c == 1 else put(6, c, left, right))
        sibling_waits.append(put(7, c, beside, sibling))
        sibling_waits.append(put(8, c, left, sibling))
        sibling_waits.append(put(9, c, right, sibling))

    for copy in text_copies[7:] + label_copies[7:]:
        copy.wait_recv()
    losses = image_batch(0)
    opposite_beside = []
    for c in each:
        beside_right[c].wait_recv()
        beside_left[c].wait_recv()
        opposite_beside.append(put(10, c, across(left), right) if c == 1 else put(10, c, across(right), left))
        sibling_waits.append(put(11, c, across(left), sibling))
        sibling_waits.append(put(12, c, across(right), sibling))
        if c + 1 < blocks // batch:
            losses = losses + image_batch(c + 1)
    for q in range(pieces + 1, blocks // batch):
        losses = losses + image_batch(q)

    for copy in to_sibling:
        copy.wait_recv()
    for copy in sibling_waits[0::3][:pieces]:
        copy.wait_recv()
    text_batch(place, True)
    for c in each:
        opposite_own[c].wait_recv()
        last_own = put(13, c, opposite, sibling)
        opposite_beside[c].wait_recv()
        last_beside = put(14, c, across(opposite), sibling)
        started_last = (last_own, last_beside)
        sibling_waits.extend(started_last)
    for copy in sibling_waits[1 : 3 * pieces : 3] + sibling_waits[2 : 3 * pieces : 3]:
        copy.wait_recv()
    for copy in sibling_waits[3 * pieces : 5 * pieces]:
        copy.wait_recv()
    text_batch(left, False)
    text_batch(right, False)
    loss_ref[...] = row_of(jnp.sum(losses, axis=1, keepdims=True))
    for copy in sibling_waits[5 * pieces :]:
        copy.wait_recv()
    text_batch(opposite, False)
    for copy in started + text_copies + label_copies:
        copy.wait_send()


def main_call(patch_rows, count_table, w_qkv_t, w_out, own_texts, labels, blocks):
    cap, dests, width = patch_rows.shape
    images = own_texts.shape[0]
    inner = HEADS * HEAD_DIM
    half = -(-width // 256) * 128
    copies = 15 * (images // PIECE)
    vmem = pl.BlockSpec(memory_space=pltpu.VMEM)
    hbm = pl.BlockSpec(memory_space=pl.ANY)
    dma = pltpu.SemaphoreType.DMA
    return pl.pallas_call(
        main_kernel,
        out_shape=(
            jax.ShapeDtypeStruct((images, width), jnp.bfloat16),
            jax.ShapeDtypeStruct((1, images), jnp.float32),
            jax.ShapeDtypeStruct((images, width), jnp.float32),
            jax.ShapeDtypeStruct((images, width), jnp.float32),
        ),
        in_specs=[hbm, vmem, hbm, hbm, vmem, vmem],
        out_specs=(vmem,) * 4,
        scratch_shapes=[
            pltpu.VMEM((cap, dests, width), jnp.bfloat16),
            pltpu.VMEM(w_qkv_t.shape, jnp.bfloat16),
            pltpu.VMEM(w_out.shape, jnp.bfloat16),
            pltpu.VMEM((cap * dests, width), jnp.bfloat16),
            pltpu.VMEM((3, cap * dests, inner), jnp.bfloat16),
            pltpu.VMEM((dests, width), jnp.float32),
            pltpu.VMEM((dests, inner), jnp.float32),
            pltpu.VMEM((dests, 2, half), jnp.float32),
            pltpu.VMEM((dests, 2, half), jnp.bfloat16),
            pltpu.VMEM((dests, 2, half), jnp.bfloat16),
            pltpu.VMEM((blocks, images, width), jnp.bfloat16),
            pltpu.VMEM((blocks, 8, 128), jnp.int32),
            pltpu.VMEM((blocks, images, width), jnp.bfloat16),
            dma((5,)),
            dma,
            dma,
            dma((30,)),
            dma((30,)),
            dma((copies,)),
            dma((copies,)),
        ],
        compiler_params=pltpu.CompilerParams(
            collective_id=0, has_side_effects=True, vmem_limit_bytes=56 * 2**20
        ),
        cost_estimate=pl.CostEstimate(flops=6 * 10**9, bytes_accessed=8 * 10**6, transcendentals=10**6),
        name="main",
    )(patch_rows, count_table, w_qkv_t, w_out, own_texts, labels)


def finish_kernel(img_ref, img_grad_ref, text_ref, text_grad_ref, loss_ref, d_img_ref, d_text_ref, losses_ref):
    for rows_ref, grad_ref, out_ref in ((img_ref, img_grad_ref, d_img_ref), (text_ref, text_grad_ref, d_text_ref)):
        rows = rows_ref[...]
        out_ref[...] = tangent(rows, inverse_norms(rows.astype(jnp.float32)), logit_scale * grad_ref[...])
    losses_ref[...] = loss_ref[...]


def finish(img, img_grad, text, text_grad, losses):
    vmem = pl.BlockSpec(memory_space=pltpu.VMEM)
    return pl.pallas_call(
        finish_kernel,
        out_shape=tuple(jax.ShapeDtypeStruct(v.shape, jnp.float32) for v in (img, text, losses)),
        in_specs=[vmem] * 5,
        out_specs=(vmem,) * 3,
        name="finish",
    )(img, img_grad, text, text_grad, losses)


def local(patches, counts, w_qkv, w_out, text_rows, labels):
    own_texts = text_rows[0]
    patch_rows = jnp.transpose(patches[0, 0], (1, 0, 2))
    img, losses, img_grad, text_grad = main_call(
        patch_rows, counts[0], w_qkv.T, w_out, own_texts, labels, lax.axis_size("blk")
    )
    d_pooled, d_texts, losses = finish(img, img_grad, own_texts, text_grad, losses)
    return (losses, d_pooled[None], d_texts[None])


def solution(mesh):
    in_specs = (
        P("blk", "dp", None, None, None),
        P("blk", None, None),
        P(),
        P(),
        P("dp", "blk", None),
        P("dp", "blk"),
    )
    out_specs = (P("dp", "blk"), P("dp", "blk", None), P("dp", "blk", None))
    return jax.shard_map(local, mesh=mesh, in_specs=in_specs, out_specs=out_specs, check_vma=False)
```

profile of v0, /device:TPU:1, one launch (start us, length us, event | category | flops | bytes accessed | tf_op | source)
XLA Modules:
  0.0 63.0 jit_solution(13436810598129156531)
XLA Ops:
  0.6 60.2 %main.1 = (bf16[48,1152]{1,0:T(8,128)(2,1)}, f32[1,48]{1,0:T(1,128)}, f32[48,1152]{1,0:T(8,128)}, f32[48,1152]{1,0:T(8,128)}) custom-call(bf16[12,64,1152]{2,1,0:T(8,128)(2,1)} %bitcast.11, s32[64,64]{1,0:T(8,128)} %bitcast.14, bf16[1728,1152]{1,0:T(8,128)(2,1)} %bitcast.10, bf16[576,1152]{1,0:T(8,128)(2,1)} %wo_hbm.1, bf16[48,1152]{1,0:T(8,128)(2,1)} %bitcast.8, ...), custom_call_target="tpu_custom_call" | custom-call | flops 6000000000 | bytes 8000000 | tf_op jit(solution)/shard_map/main/pallas_call | solution.py:361
  60.9 2.2 %finish.1 = (f32[48,1152]{1,0:T(8,128)}, f32[48,1152]{1,0:T(8,128)}, f32[1,48]{1,0:T(1,128)}) custom-call(bf16[48,1152]{1,0:T(8,128)(2,1)} %get-tuple-element.10.img_ref, f32[48,1152]{1,0:T(8,128)} %get-tuple-element.11.img_grad_ref, bf16[48,1152]{1,0:T(8,128)(2,1)} %bitcast.9, f32[48,1152]{1,0:T(8,128)} %get-tuple-element.12.text_grad_ref, ...), custom_call_target="tpu_custom_call" | custom-call | tf_op jit(solution)/shard_map/finish/pallas_call | solution.py:410
where the time goes:
time: 63.2 us; the launch traced here: 63 us
  Pallas kernels  62.4 us (99%)
  between operations  0.64 us (1%)
    pallas_call x1, Pallas kernels, main_call(): pl.pallas_call(main_kernel, out_shape=(jax.ShapeDtypeStruct((images, widt...  60.2 us
    pallas_call x1, Pallas kernels, finish(): pl.pallas_call(finish_kernel, out_shape=tuple((jax.ShapeDtypeStruct(v.sha...  2.15 us

commit v1 on v0

--- a/solution.py
+++ b/solution.py
@@ -78,8 +78,8 @@
 
     beside = across(place)
     right, left, opposite = (lax.rem(place + 4 * step, blocks) for step in (1, 3, 2))
-    peers = (opposite, across(opposite), across(right), across(left), right, left, beside)
-    mirror = (0, 1, 3, 2, 5, 4, 6)
+    targets = (across(right), across(left), right, left, beside, sibling)
+    sources = (across(left), across(right), left, right, beside, sibling)
     cap, dests, width = patch_ref.shape
     inner = HEADS * HEAD_DIM
     rows = cap * SUBGROUP
@@ -103,7 +103,7 @@
         return carry
 
     lax.fori_loop(1, dests, greet, 0)
-    for neighbour in (sibling,) + peers:
+    for neighbour in targets:
         pl.semaphore_signal(barrier, inc=1, device_id={"blk": neighbour}, device_id_type=MESH)
 
     texts_ref[place] = text_ref[...]
@@ -137,6 +137,22 @@
             normed_ref[...], wt_ref[p * inner : (p + 1) * inner, :], NT, preferred_element_type=jnp.float32
         ).astype(jnp.bfloat16)
     loads[4].wait()
+
+    pl.semaphore_wait(barrier, dests - 1 + len(targets))
+    text_copies, label_copies = [], []
+
+    def pass_text(k, block, to):
+        for ref, sems, copies in ((texts_ref, 0, text_copies), (labels_ref, 15, label_copies)):
+            spot = ref.at[block]
+            copy = pltpu.make_async_remote_copy(
+                spot, spot, text_send_sems.at[sems + k], text_recv_sems.at[sems + k],
+                device_id={"blk": to}, device_id_type=MESH,
+            )
+            copy.start()
+            copies.append(copy)
+
+    for k, to in enumerate(targets):
+        pass_text(k, place, to)
 
     query_id = lax.broadcasted_iota(jnp.int32, (rows, rows), 0)
     key_id = lax.broadcasted_iota(jnp.int32, (rows, rows), 1)
@@ -175,18 +191,6 @@
         mixed = jnp.dot(stacked, packed_ref[2, group_rows, :], preferred_element_type=jnp.float32)
         return jnp.sum(mixed.reshape(HEADS, SUBGROUP, inner) * head_mask, axis=0)
 
-    text_copies, label_copies = [], []
-
-    def pass_text(k, block, to):
-        for ref, sems, copies in ((texts_ref, 0, text_copies), (labels_ref, 15, label_copies)):
-            spot = ref.at[block]
-            copy = pltpu.make_async_remote_copy(
-                spot, spot, text_send_sems.at[sems + k], text_recv_sems.at[sems + k],
-                device_id={"blk": to}, device_id_type=MESH,
-            )
-            copy.start()
-            copies.append(copy)
-
     for members in (range(groups - 1), range(groups - 1, groups)):
         for k in members:
             pool_ref[k * SUBGROUP : (k + 1) * SUBGROUP, :] = pool_group(k)
@@ -195,8 +199,6 @@
         wide_ref[span, 0, :] = result[:, :half]
         filler = jnp.zeros((result.shape[0], 2 * half - width), jnp.float32)
         wide_ref[span, 1, :] = jnp.concatenate([result[:, half:], filler], axis=1)
-        if members[0] == 0:
-            pl.semaphore_wait(barrier, dests - 1 + 1 + len(peers))
         for k in members:
             base = order[k] * SUBGROUP
             sent_ref[pl.ds(base, SUBGROUP)] = wide_ref[k * SUBGROUP : (k + 1) * SUBGROUP].astype(jnp.bfloat16)
@@ -209,10 +211,21 @@
                 return carry
 
             lax.fori_loop(1 if k == groups - 1 else 0, SUBGROUP, send, 0)
-        if members[0] == 0:
-            for k, to in enumerate(peers + (sibling,)):
-                pass_text(k, place, to)
     arrived_ref[me] = sent_ref[me]
+
+    def take_text(k):
+        text_copies[k].wait_recv()
+        label_copies[k].wait_recv()
+
+    take_text(2)
+    pass_text(6, left, right)
+    take_text(1)
+    pass_text(7, across(right), left)
+    pass_text(8, left, sibling)
+    pass_text(9, across(right), sibling)
+    for k in (4, 3, 0):
+        take_text(k)
+        pass_text({4: 10, 3: 11, 0: 12}[k], sources[k], sibling)
 
     lane = lax.broadcasted_iota(jnp.int32, (dests, dests), 1)
     sublane = lax.broadcasted_iota(jnp.int32, (dests, dests), 0)
@@ -225,6 +238,11 @@
 
     batch = 4
     wide = batch * images
+
+    take_text(6)
+    pass_text(13, opposite, sibling)
+    take_text(7)
+    pass_text(14, across(opposite), sibling)
 
     pltpu.make_async_remote_copy(
         sent_ref.at[pl.ds(0, dests - 1)], arrived_ref.at[pl.ds(0, dests - 1)], send_sem, recv_sem,
@@ -290,11 +308,6 @@
     to_left = [put(1, c, place, left) for c in each]
     to_beside = [put(2, c, place, beside) for c in each]
     to_sibling = [put(3, c, place, sibling) for c in each]
-    for k in (6, 4, 5, 2, 3, 0, 1):
-        text_copies[k].wait_recv()
-        label_copies[k].wait_recv()
-        pass_text(8 + k, peers[mirror[k]], sibling)
-
     sibling_waits = []
     beside_right, beside_left, opposite_own = [], [], []
     for c in each:
@@ -308,8 +321,8 @@
         sibling_waits.append(put(8, c, left, sibling))
         sibling_waits.append(put(9, c, right, sibling))
 
-    for copy in text_copies[7:] + label_copies[7:]:
-        copy.wait_recv()
+    for k in (5, 8, 9, 10, 11, 12, 13, 14):
+        take_text(k)
     losses = image_batch(0)
     opposite_beside = []
     for c in each:

time: 63.2 us -> 63 us (level)
  no operation moved by 1% of the time
where the time goes in v1:
time: 63 us; the launch traced here: 62.8 us
  Pallas kernels  62.1 us (99%)
  between operations  0.64 us (1%)
    pallas_call x1, Pallas kernels, main_call(): pl.pallas_call(main_kernel, out_shape=(jax.ShapeDtypeStruct((images, widt...  60 us
    pallas_call x1, Pallas kernels, finish(): pl.pallas_call(finish_kernel, out_shape=tuple((jax.ShapeDtypeStruct(v.sha...  2.15 us

profile of v1, /device:TPU:1, one launch (start us, length us, event | category | flops | bytes accessed | tf_op | source)
XLA Modules:
  0.0 62.8 jit_solution(18274641584593096209)
XLA Ops:
  0.6 60.0 %main.1 = (bf16[48,1152]{1,0:T(8,128)(2,1)}, f32[1,48]{1,0:T(1,128)}, f32[48,1152]{1,0:T(8,128)}, f32[48,1152]{1,0:T(8,128)}) custom-call(bf16[12,64,1152]{2,1,0:T(8,128)(2,1)} %bitcast.11, s32[64,64]{1,0:T(8,128)} %bitcast.14, bf16[1728,1152]{1,0:T(8,128)(2,1)} %bitcast.10, bf16[576,1152]{1,0:T(8,128)(2,1)} %wo_hbm.1, bf16[48,1152]{1,0:T(8,128)(2,1)} %bitcast.8, ...), custom_call_target="tpu_custom_call" | custom-call | flops 6000000000 | bytes 8000000 | tf_op jit(solution)/shard_map/main/pallas_call | solution.py:374
  60.6 2.2 %finish.1 = (f32[48,1152]{1,0:T(8,128)}, f32[48,1152]{1,0:T(8,128)}, f32[1,48]{1,0:T(1,128)}) custom-call(bf16[48,1152]{1,0:T(8,128)(2,1)} %get-tuple-element.10.img_ref, f32[48,1152]{1,0:T(8,128)} %get-tuple-element.11.img_grad_ref, bf16[48,1152]{1,0:T(8,128)(2,1)} %bitcast.9, f32[48,1152]{1,0:T(8,128)} %get-tuple-element.12.text_grad_ref, ...), custom_call_target="tpu_custom_call" | custom-call | tf_op jit(solution)/shard_map/finish/pallas_call | solution.py:423
